TPU v7x, 128 devices: a whole 4x4x4 slice. The times are simulated.
128 devices in a mesh: ctx: 16 (over x, z), pp: 4 (over y_lo, core), tp: 2 (over y_hi).
Axes of the slice: x: 4, y: 4 (y_hi: 2, y_lo: 2; y = y_hi * 2 + y_lo), z: 4, core: 2. Of those that a mesh axis runs over, the one named last changes fastest.
Arguments:
- next_grad: bfloat16 [4, 2048, 6144], P('pp', ('ctx', 'tp')), may hold values from -6 to 6
- queries: bfloat16 [4, 2048, 6144], P('pp', 'ctx', 'tp'), may hold values from -6 to 6
- keys: bfloat16 [4, 2048, 6144], P('pp', 'ctx', 'tp'), may hold values from -6 to 6
- values: bfloat16 [4, 2048, 6144], P('pp', 'ctx', 'tp'), may hold values from -6 to 6
- outputs: bfloat16 [4, 2048, 6144], P('pp', 'ctx', 'tp'), may hold values from -6 to 6
- log_sums: float32 [4, 2048, 48], P('pp', 'ctx', 'tp'), may hold values from 4 to 7
- part_length: int32 [4], P('pp'), may hold values from 64 to 1984, as said below
Outputs:
- query_grad: bfloat16 [4, 2048, 6144], P('pp', 'ctx', 'tp')
- key_grad: bfloat16 [4, 2048, 6144], P('pp', 'ctx', 'tp')
- value_grad: bfloat16 [4, 2048, 6144], P('pp', 'ctx', 'tp')
Inputs may be any that keep to these rules, and one draw needn't show every extreme that they name: `part_length`: each section's sequence has its own part-A length; the shortest and the longest allowed both occur in every draw.
All inputs are finite; a program needn't handle non-finite values.
Results may differ from a plain program's by a relative error of at most 0.0051.
Values may be sent and summed in bfloat16 or wider, within the bound.
No kernel may reach another device: no remote copies, remote signals or barrier semaphores. Data moves between devices by JAX's collectives and lax.ppermute only.
A program may use at most 192 MiB of HBM per device.

v0:
```python
import jax
import jax.numpy as jnp
from jax import lax
from jax.sharding import PartitionSpec as P

HDIM = 128


def from_behind(block, axis, distance):
    devices = range(lax.axis_size(axis))
    route = [((i - distance) % len(devices), i) for i in devices]
    return lax.ppermute(block, axis, route)


def visible_any(query_pos, key_pos, part_len):
    lowest_key = jnp.min(key_pos)
    return jnp.logical_or(lowest_key < part_len, lowest_key <= jnp.max(query_pos))


def tile_terms(
    query_tile,
    grad_tile,
    sum_tile,
    delta_tile,
    key_tile,
    value_tile,
    query_pos,
    key_pos,
    part_len,
    factor,
):
    visible = jnp.logical_or(key_pos[None, :] < part_len, key_pos[None, :] <= query_pos[:, None])
    scores = (
        jnp.einsum("qhd,khd->hqk", query_tile, key_tile, preferred_element_type=jnp.float32)
        * factor
    )
    weights = jnp.where(visible[None], jnp.exp(scores - jnp.transpose(sum_tile)[:, :, None]), 0.0)
    weight_grads = jnp.einsum(
        "qhd,khd->hqk", grad_tile, value_tile, preferred_element_type=jnp.float32
    )
    score_grads = (
        weights * (weight_grads - jnp.transpose(delta_tile)[:, :, None]) * factor
    ).astype(jnp.bfloat16)
    return (weights, score_grads)


def add_query_grads(asking, key_piece, value_piece, query_pos, key_pos, part_len, factor):
    query_rows, grad_rows, sum_rows, delta_rows = asking

    def compute():
        weights, score_grads = tile_terms(
            query_rows,
            grad_rows,
            sum_rows,
            delta_rows,
            key_piece,
            value_piece,
            query_pos,
            key_pos,
            part_len,
            factor,
        )
        return jnp.einsum(
            "hqk,khd->qhd", score_grads, key_piece, preferred_element_type=jnp.float32
        )

    def skipped():
        return jnp.zeros(query_rows.shape, jnp.float32)

    return lax.cond(visible_any(query_pos, key_pos, part_len), compute, skipped)


def add_key_grads(key_rows, value_rows, asking, query_pos, key_pos, part_len, factor):
    query_piece, grad_piece, sum_piece, delta_piece = asking

    def compute():
        weights, score_grads = tile_terms(
            query_piece,
            grad_piece,
            sum_piece,
            delta_piece,
            key_rows,
            value_rows,
            query_pos,
            key_pos,
            part_len,
            factor,
        )
        key_term = jnp.einsum(
            "hqk,qhd->khd", score_grads, query_piece, preferred_element_type=jnp.float32
        )
        value_term = jnp.einsum(
            "hqk,qhd->khd",
            weights.astype(jnp.bfloat16),
            grad_piece,
            preferred_element_type=jnp.float32,
        )
        return (key_term, value_term)

    def skipped():
        empty = jnp.zeros(key_rows.shape, jnp.float32)
        return (empty, empty)

    key_term, value_term = lax.cond(visible_any(query_pos, key_pos, part_len), compute, skipped)
    return (key_term, value_term)


def per_device(next_grad, queries, keys, values, outputs, log_sums, part_length):
    incoming = from_behind(next_grad, "pp", -1)
    grad_out = lax.all_to_all(incoming, "tp", split_axis=2, concat_axis=1, tiled=True)
    seq_rows = queries.shape[1]
    width = queries.shape[2]
    local_heads = width // HDIM
    self_index = lax.axis_index("ctx")
    part_len = part_length[0]
    factor = HDIM ** (-0.5)
    shape_three = (seq_rows, local_heads, HDIM)
    query_rows = queries.reshape(shape_three)
    key_rows = keys.reshape(shape_three)
    value_rows = values.reshape(shape_three)
    grad_rows = grad_out.reshape(shape_three)
    deltas = jnp.sum(
        grad_rows.astype(jnp.float32) * outputs.reshape(shape_three).astype(jnp.float32), axis=2
    )
    sum_rows = log_sums.reshape(seq_rows, local_heads)
    local_index = jnp.arange(seq_rows, dtype=jnp.int32)
    own_pos = self_index * seq_rows + local_index
    all_sums, all_deltas = (
        lax.all_gather(sum_rows, "ctx", axis=0, tiled=True),
        lax.all_gather(deltas, "ctx", axis=0, tiled=True),
    )
    asking = (query_rows, grad_rows, sum_rows, deltas)
    key_piece = lax.all_gather(key_rows, "ctx", axis=0, tiled=True)
    value_piece = lax.all_gather(value_rows, "ctx", axis=0, tiled=True)
    count = key_piece.shape[0]
    piece_pos = jnp.arange(count, dtype=jnp.int32)
    query_total = add_query_grads(
        asking, key_piece, value_piece, own_pos, piece_pos, part_len, factor
    )
    query_piece = lax.all_gather(query_rows, "ctx", axis=0, tiled=True)
    grad_piece = lax.all_gather(grad_rows, "ctx", axis=0, tiled=True)
    count = query_piece.shape[0]
    piece_pos = jnp.arange(count, dtype=jnp.int32)
    key_total, value_total = add_key_grads(
        key_rows,
        value_rows,
        (query_piece, grad_piece, all_sums, all_deltas),
        piece_pos,
        own_pos,
        part_len,
        factor,
    )
    query_low = query_total.astype(jnp.bfloat16).reshape(seq_rows, width)
    key_low = key_total.astype(jnp.bfloat16).reshape(seq_rows, width)
    value_low = value_total.astype(jnp.bfloat16).reshape(seq_rows, width)
    return (
        query_low.reshape(1, seq_rows, width),
        key_low.reshape(1, seq_rows, width),
        value_low.reshape(1, seq_rows, width),
    )


def solution(mesh):
    placed = (
        P("pp", ("ctx", "tp"), None),
        P("pp", "ctx", "tp"),
        P("pp", "ctx", "tp"),
        P("pp", "ctx", "tp"),
        P("pp", "ctx", "tp"),
        P("pp", "ctx", "tp"),
        P("pp"),
    )
    return jax.shard_map(
        per_device,
        mesh=mesh,
        in_specs=placed,
        out_specs=(P("pp", "ctx", "tp"), P("pp", "ctx", "tp"), P("pp", "ctx", "tp")),
        check_vma=False,
    )
```

profile of v0, /device:TPU:24, one launch (start us, length us, event | category | flops | bytes accessed | tf_op | source)
XLA Modules:
  0.0 488.6 jit_solution(10878357510282478842)
XLA Ops:
  7.2 2.3 copy.71
  9.6 2.2 copy.98
  11.9 2.3 copy.70
  14.5 9.8 %collective-permute-done = bf16[1,64,6144]{2,1,0:T(8,128)(2,1)} collective-permute-done((bf16[1,64,6144]{2,1,0:T(8,128)(2,1)}, bf16[1,64,6144]{2,1,0:T(8,128)(2,1)}, u32[]{:S(2)}, u32[]{:S(2)}) %collective-permute-start) | collective-permute-done | bytes 786464 | tf_op jit(solution)/shard_map/ppermute | solution.py:12
  24.3 6.7 %copy.72 = bf16[1,64,6144]{1,0,2:T(2,128)(2,1)S(1)} copy(bf16[1,64,6144]{2,1,0:T(8,128)(2,1)} %collective-permute-done) | data formatting | bytes 1572864 | tf_op jit(solution)/shard_map/ppermute | solution.py:12
  31.5 34.4 %reduce = bf16[6144,64]{1,0:T(8,128)(2,1)} reduce(bf16[6144,1,64]{2,1,0:T(2,128)(2,1)S(1)} %bitcast.50, bf16[]{:T(256)} %broadcast.99), dimensions={1}, to_apply=%bitcast.30.reduce_sub_computation | reduce | bytes 1572866
  66.0 2.4 reshape.128
  68.3 14.3 %all_to_all.15 = bf16[2,2,98304]{2,1,0:T(2,128)(2,1)} all-to-all(bf16[2,2,98304]{2,1,0:T(2,128)(2,1)S(1)} %reshape.128), channel_id=1, replica_groups=mesh['ctx'=16,'pp'=4,'tp'=2] {'tp'}, dimensions={0} | all-to-all | bytes 1572864 | tf_op jit(solution)/shard_map/all_to_all | solution.py:110
  82.6 2.2 reshape.129
  84.9 4.9 copy.73
  89.8 2.7 all_to_all.12
  92.6 1.0 copy.97
  95.6 1.3 convert_bitcast_fusion
  98.6 26.8 %all-gather = f32[1,2048,24]{1,2,0:T(8,128)} all-gather(f32[1,128,24]{1,2,0:T(8,128)S(1)} %copy-done.5), channel_id=2, replica_groups=mesh['ctx'=16,'pp'=4,'tp'=2] {'ctx'}, dimensions={1}, use_global_device_ids=true | all-gather | bytes 208896 | tf_op jit(solution)/shard_map/all_gather | solution.py:129
  125.4 1.8 multiply_reduce_fusion
  127.2 25.6 %all_gather.23 = f32[2048,24]{1,0:T(8,128)S(1)} all-gather(f32[128,24]{1,0:T(8,128)S(1)} %multiply_reduce_fusion), channel_id=1, replica_groups=mesh['ctx'=16,'pp'=4,'tp'=2] {'ctx'}, dimensions={0}, use_global_device_ids=true | all-gather | bytes 208896 | tf_op jit(solution)/shard_map/all_gather | solution.py:130
  152.8 55.0 %all-gather.8.cloned.1.call-done = bf16[2048,24,128]{2,1,0:T(8,128)(2,1)} async-done(((bf16[128,24,128]{2,1,0:T(8,128)(2,1)}), bf16[2048,24,128]{2,1,0:T(8,128)(2,1)}) %all-gather.8.cloned.1.call-update) | async-done | bytes 12582928 | tf_op jit(solution)/shard_map/all_gather | solution.py:134
  207.7 44.2 %conditional.2 = (bf16[1,128,3072]{2,1,0:T(8,128)(2,1)}) conditional(s32[]{:T(128)} %convert_element_type.58, () %tuple.28, (s32[]{:T(128)}, s32[2048]{0:T(1024)S(1)}, s32[2048]{0:T(1024)S(1)}, s32[128]{0:T(128)S(1)}, bf16[128,24,128]{0,2,1:T(8,128)(2,1)S(1)}, /*index=5*/bf16[2048,24,128]{0,2,1:T(8,128)(2,1)}, f32[128,24]{0,1:T(8,128)S(1)}, ...), branch_computations={%region_2.0_spmd, %region_3.0_spmd} | conditional | flops 4876797952 | bytes 80024072 | solution.py:70
  207.8 15.2 %fusion = f32[24,128,2048]{2,1,0:T(8,128)} fusion(bf16[2048,24,128]{2,1,0:T(8,128)(2,1)} %get-tuple-element.156, bf16[128,24,128]{2,1,0:T(8,128)(2,1)} %get-tuple-element.155), kind=kOutput, calls=%fused_computation.1 | convolution fusion | flops 1610612736 | bytes 38535168 | tf_op jit(solution)/shard_map/cond/branch_1_fun/qhd,khd->hqk/dot_general | solution.py:38
  223.7 0.9 compare_or_fusion
  224.7 24.9 %fusion.6 = bf16[24,128,128]{1,2,0:T(8,128)(2,1)} fusion(bf16[2048,24,128]{0,2,1:T(8,128)(2,1)} %get-tuple-element.48, f32[24,128,2048]{2,1,0:T(8,128)} %fusion, f32[24,128]{1,0:T(8,128)S(1)} %bitcast.71, f32[24,128]{1,0:T(8,128)S(1)} %bitcast.70, bf16[128,24,128]{0,2,1:T(8,128)(2,1)S(1)} %get-tuple-element.152, pred[128,2048]{1,0:T(8,128)(4,1)} %compare_or_fusion), kind=kOutput, calls=%fused_computation.6 | convolution fusion | flops 3265658880 | bytes 39608320 | tf_op jit(solution)/shard_map/cond/branch_1_fun/hqk,khd->qhd/dot_general | solution.py:63
  249.6 2.3 copy.92
  251.9 58.0 %all-gather.10.cloned.1.call-done = bf16[2048,24,128]{0,2,1:T(8,128)(2,1)} async-done(((bf16[128,24,128]{0,2,1:T(8,128)(2,1)}), bf16[2048,24,128]{0,2,1:T(8,128)(2,1)}) %all-gather.10.cloned.1.call-update) | async-done | bytes 12582928 | tf_op jit(solution)/shard_map/all_gather | solution.py:140
  309.9 91.5 %all-gather.12.cloned.1.call-done = bf16[2048,24,128]{2,1,0:T(8,128)(2,1)} async-done(((bf16[128,24,128]{2,1,0:T(8,128)(2,1)}), bf16[2048,24,128]{2,1,0:T(8,128)(2,1)}) %all-gather.12.cloned.1.call-update) | async-done | bytes 12582928 | tf_op jit(solution)/shard_map/all_gather | solution.py:141
  401.4 79.9 %conditional.3 = (bf16[1,128,3072]{2,1,0:T(8,128)(2,1)S(1)}, bf16[1,128,3072]{2,1,0:T(8,128)(2,1)}) conditional(s32[]{:T(128)} %convert_element_type.62, () %tuple.30, (s32[]{:T(128)}, s32[128]{0:T(128)S(1)}, s32[2048]{0:T(1024)S(1)}, bf16[2048,24,128]{0,2,1:T(8,128)(2,1)}, bf16[128,24,128]{0,2,1:T(8,128)(2,1)S(1)}, /*index=5*/f32[2048,24]{0,1:T(8,128)}, ...), branch_computations={%region_5.6_spmd, %region_6.7_spmd} | conditional | flops 6512967680 | bytes 185017648 | solution.py:104
  401.4 13.0 %fusion.33 = f32[24,2048,128]{2,1,0:T(8,128)} fusion(bf16[2048,24,128]{0,2,1:T(8,128)(2,1)} %get-tuple-element.56, bf16[128,24,128]{0,2,1:T(8,128)(2,1)S(1)} %get-tuple-element.162), kind=kOutput, calls=%fused_computation.37 | convolution fusion | flops 1610612736 | bytes 38535168 | tf_op jit(solution)/shard_map/cond/branch_1_fun/qhd,khd->hqk/dot_general | solution.py:34
  415.7 16.5 %copy.80 = bf16[2048,24,128]{0,2,1:T(8,128)(2,1)} copy(bf16[2048,24,128]{2,1,0:T(8,128)(2,1)} %get-tuple-element.164) | data formatting | bytes 25165824 | tf_op jit(solution)/shard_map
  432.1 20.8 %multiply_convert_fusion.10 = bf16[24,2048,128]{2,1,0:T(8,128)(2,1)} fusion(f32[24,2048,128]{2,1,0:T(8,128)} %fusion.33, f32[24,2048]{1,0:T(8,128)S(1)} %bitcast.65, f32[24,2048]{1,0:T(8,128)S(1)} %bitcast.67, pred[2048,128]{1,0:T(8,128)(4,1)S(1)} %compare_or_fusion.1, bf16[2048,24,128]{0,2,1:T(8,128)(2,1)} %copy.80, ...), kind=kOutput, calls=%fused_computation.12.clone.clone.clone.clone.1 | convolution fusion | flops 1654652928 | bytes 51773440 | tf_op jit(solution)/shard_map/cond/branch_1_fun/qhd,khd->hqk/dot_general | solution.py:38
  452.9 11.6 %fusion.21 = bf16[24,128,128]{1,2,0:T(8,128)(2,1)S(1)} fusion(bf16[2048,24,128]{0,2,1:T(8,128)(2,1)} %get-tuple-element.56, bf16[24,2048,128]{2,1,0:T(8,128)(2,1)} %multiply_convert_fusion.10), kind=kOutput, calls=%fused_computation.23 | convolution fusion | flops 1611005952 | bytes 25952256 | tf_op jit(solution)/shard_map/cond/branch_1_fun/hqk,qhd->khd/dot_general | solution.py:89
  464.8 15.3 %fusion.22 = bf16[24,128,128]{1,2,0:T(8,128)(2,1)S(1)} fusion(bf16[2048,24,128]{0,2,1:T(8,128)(2,1)} %copy.80, f32[24,2048,128]{2,1,0:T(8,128)} %fusion.33, f32[24,2048]{1,0:T(8,128)S(1)} %bitcast.68, pred[2048,128]{1,0:T(8,128)(4,1)S(1)} %compare_or_fusion.1), kind=kOutput, calls=%fused_computation.24 | convolution fusion | flops 1636171776 | bytes 38993920 | tf_op jit(solution)/shard_map/cond/branch_1_fun/hqk,qhd->khd/dot_general | solution.py:92
  480.1 1.2 copy.96
  481.2 0.9 copy-done.3
  (34 shorter events, 4.5 us)
Async XLA Ops:
  7.2 145.6 %all-gather.6.cloned.1.call-start = ((), (), s32[]{:S(2)}) async-start(), calls=%async_computation.1 | async-start | bytes 13369344 | tf_op jit(solution)/shard_map/all_gather | solution.py:133
  9.5 198.2 %all-gather.8.cloned.1.call-start = ((), (), s32[]{:S(2)}) async-start(), calls=%async_computation.2 | async-start | bytes 13369344 | tf_op jit(solution)/shard_map/all_gather | solution.py:134
  11.8 298.0 %all-gather.10.cloned.1.call-start = ((), (), s32[]{:S(2)}) async-start(), calls=%async_computation.3 | async-start | bytes 13369344 | tf_op jit(solution)/shard_map/all_gather | solution.py:140
  14.2 387.2 %all-gather.12.cloned.1.call-start = ((), (), s32[]{:S(2)}) async-start(), calls=%async_computation.4 | async-start | bytes 13369344 | tf_op jit(solution)/shard_map/all_gather | solution.py:141
  14.2 10.1 %collective-permute-start = (bf16[1,64,6144]{2,1,0:T(8,128)(2,1)}, bf16[1,64,6144]{2,1,0:T(8,128)(2,1)}, u32[]{:S(2)}, u32[]{:S(2)}) collective-permute-start(bf16[1,64,6144]{2,1,0:T(8,128)(2,1)} %param.11), channel_id=1, source_target_pairs={{2,0},{4,2},{6,4},{0,6},{3,1},{5,3},{7,5},{1,7},{10,8},{12,10},{14... | collective-permute-start | bytes 2359304 | tf_op jit(solution)/shard_map/ppermute | solution.py:12
  66.0 32.7 %copy-start.5 = (f32[1,128,24]{1,2,0:T(8,128)S(1)}, f32[1,128,24]{1,2,0:T(8,128)}, u32[]{:S(2)}) copy-start(f32[1,128,24]{1,2,0:T(8,128)} %param.16) | copy-start | bytes 36868
  89.8 118.0 %copy-start.2 = (bf16[1,128,3072]{1,2,0:T(8,128)(2,1)S(1)}, bf16[1,128,3072]{1,2,0:T(8,128)(2,1)}, u32[]{:S(2)}) copy-start(bf16[1,128,3072]{1,2,0:T(8,128)(2,1)} %copy.70) | copy-start | bytes 2359300
  207.7 193.6 %copy-start = (bf16[1,128,3072]{1,2,0:T(8,128)(2,1)S(1)}, bf16[1,128,3072]{1,2,0:T(8,128)(2,1)}, u32[]{:S(2)}) copy-start(bf16[1,128,3072]{1,2,0:T(8,128)(2,1)} %copy.71) | copy-start | bytes 2359300
  207.7 193.6 %copy-start.1 = (bf16[16,8,24,128]{3,2,1,0:T(8,128)(2,1)S(1)}, bf16[16,8,24,128]{3,2,1,0:T(8,128)(2,1)}, u32[]{:S(2)}) copy-start(bf16[16,8,24,128]{3,2,1,0:T(8,128)(2,1)} %copy.98) | copy-start | bytes 2359300
  415.7 16.5 %copy-start.4 = (f32[2048,24]{0,1:T(8,128)S(1)}, f32[2048,24]{0,1:T(8,128)}, u32[]{:S(2)}) copy-start(f32[2048,24]{0,1:T(8,128)} %get-tuple-element.58) | copy-start | bytes 589828 | tf_op jit(solution)/shard_map/cond
  481.2 0.9 copy-start.3
Sparse Core Ops, SparseCore 0:
  10.7 102.1 all-gather.5
  115.1 92.5 all-gather.7
  210.4 99.4 all-gather.9
  311.9 89.4 all-gather.11
where the time goes:
time: 491 us; the launch traced here: 489 us
  waiting for transfers between devices  214 us (44%)
  matrix products  101 us (21%)
  blocking collectives  66.7 us (14%)
  local copies, waits for them, and re-layouts  49 us (10%)
  other arithmetic  40.9 us (8%)
  between operations  16.5 us (3%)
    all_gather x1, waiting for transfers between devices, per_device(): grad_piece = lax.all_gather(grad_rows, 'ctx', axis=0, tiled=True)  91.5 us
    all_gather x1, waiting for transfers between devices, per_device(): query_piece = lax.all_gather(query_rows, 'ctx', axis=0, tiled=True)  58 us
    all_gather x1, waiting for transfers between devices, per_device(): value_piece = lax.all_gather(value_rows, 'ctx', axis=0, tiled=True)  55 us
    dot_general x2, matrix products, tile_terms(): jnp.einsum('qhd,khd->hqk', grad_tile, value_tile, preferred_element_type=...  36 us
    unnamed x2, other arithmetic  35.8 us
    all_gather x1, blocking collectives, per_device(): lax.all_gather(sum_rows, 'ctx', axis=0, tiled=True)  26.8 us
    all_gather x1, blocking collectives, per_device(): lax.all_gather(deltas, 'ctx', axis=0, tiled=True)  25.6 us
    dot_general x1, matrix products, compute(): jnp.einsum('hqk,khd->qhd', score_grads, key_piece, preferred_element_type...  24.9 us
  transfers between devices with their start and end apart: 5, of which 4 were waited for; matrix products, arithmetic and copies ran while one was open for 21% of the time, Pallas kernels for 0%

commit v1 on v0

v1 whole, which is shorter than its diff:
```python
import functools

import jax
import jax.numpy as jnp
from jax import lax
from jax.experimental import pallas as pl
from jax.experimental.pallas import tpu as pltpu
from jax.sharding import PartitionSpec as P

HDIM = 128
LOG2E = 1.4426950408889634
FACTOR = HDIM ** (-0.5)
QTILE = 512
KTILE = 1024


def dot_nt(a, b):
    return lax.dot_general(a, b, (((1,), (1,)), ((), ())), preferred_element_type=jnp.float32)


def dot_nn(a, b):
    return lax.dot_general(a, b, (((1,), (0,)), ((), ())), preferred_element_type=jnp.float32)


def dot_tn(a, b):
    return lax.dot_general(a, b, (((0,), (0,)), ((), ())), preferred_element_type=jnp.float32)


def attention_kernel(meta_ref, qkv, grads, stat, out, dq_acc, dk_acc, dv_acc, *, blocks, seq):
    part_len = meta_ref[0]
    half = meta_ref[1]
    span = QTILE // seq
    query_tiles = blocks // span

    def one_head(rows, q_at, k_at, v_at, g_at, which, dq_at, dk_at, dv_at):
        key_span = KTILE // rows
        dq_acc[...] = jnp.zeros_like(dq_acc)

        def key_tile(kt, carry):
            first = kt * key_span
            key_rows = qkv[pl.ds(first, key_span), k_at : k_at + rows, :].reshape(KTILE, HDIM)
            value_rows = qkv[pl.ds(first, key_span), v_at : v_at + rows, :].reshape(KTILE, HDIM)
            index = lax.broadcasted_iota(jnp.int32, (KTILE, 1), 0)
            if rows == seq:
                key_pos = first * seq + index
            else:
                key_pos = (first + index // rows) * seq + half * rows + index % rows
            key_pos = jnp.where(key_pos < part_len, -1, key_pos)
            dk_acc[...] = jnp.zeros_like(dk_acc)
            dv_acc[...] = jnp.zeros_like(dv_acc)

            def query_tile(qt, carry):
                at = qt * span
                query_rows = qkv[pl.ds(at, span), q_at : q_at + seq, :].reshape(QTILE, HDIM)
                grad_rows = grads[pl.ds(at, span), g_at : g_at + seq, :].reshape(QTILE, HDIM)
                log_sum = stat[2 * which, pl.ds(qt, 1), :]
                delta = stat[2 * which + 1, pl.ds(qt, 1), :]
                scores = dot_nt(key_rows, query_rows) * (FACTOR * LOG2E) - log_sum
                query_pos = at * seq + lax.broadcasted_iota(jnp.int32, (1, QTILE), 1)
                weights = jnp.where(key_pos <= query_pos, jnp.exp2(scores), 0.0)
                weight_grads = dot_nt(value_rows, grad_rows)
                score_grads = (weights * (weight_grads - delta) * FACTOR).astype(jnp.bfloat16)
                dv_acc[...] += dot_nn(weights.astype(jnp.bfloat16), grad_rows)
                dk_acc[...] += dot_nn(score_grads, query_rows)
                where = pl.ds(pl.multiple_of(at * seq, QTILE), QTILE)
                dq_acc[where, :] += dot_tn(score_grads, key_rows)
                return carry

            lax.fori_loop(0, query_tiles, query_tile, 0)
            shape = (key_span, rows, HDIM)
            out[pl.ds(first, key_span), dk_at : dk_at + rows, :] = dk_acc[...].astype(jnp.bfloat16).reshape(shape)
            out[pl.ds(first, key_span), dv_at : dv_at + rows, :] = dv_acc[...].astype(jnp.bfloat16).reshape(shape)
            return carry

        lax.fori_loop(0, blocks // key_span, key_tile, 0)
        out[:, dq_at : dq_at + seq, :] = dq_acc[...].astype(jnp.bfloat16).reshape(blocks, seq, HDIM)

    half_rows = seq // 2
    one_head(seq, 0, seq, 2 * seq, 0, 0, 0, seq, 2 * seq)
    one_head(half_rows, 3 * seq, 4 * seq, 4 * seq + half_rows, seq, 1, 3 * seq, 4 * seq, 4 * seq + half_rows)


def attention(meta, qkv, grads, stat):
    blocks = qkv.shape[0]
    seq = qkv.shape[1] // 5
    total = blocks * seq
    tiles = stat.reshape(4, total // QTILE, QTILE)
    return pl.pallas_call(
        functools.partial(attention_kernel, blocks=blocks, seq=seq),
        out_shape=jax.ShapeDtypeStruct((blocks, 5 * seq, HDIM), jnp.bfloat16),
        in_specs=[pl.BlockSpec(memory_space=pltpu.SMEM)] + [pl.BlockSpec(memory_space=pltpu.VMEM)] * 3,
        out_specs=pl.BlockSpec(memory_space=pltpu.VMEM),
        scratch_shapes=[
            pltpu.VMEM((total, HDIM), jnp.float32),
            pltpu.VMEM((KTILE, HDIM), jnp.float32),
            pltpu.VMEM((KTILE, HDIM), jnp.float32),
        ],
        compiler_params=pltpu.CompilerParams(vmem_limit_bytes=48 << 20),
        cost_estimate=pl.CostEstimate(
            flops=15 * total * total * HDIM, bytes_accessed=8 << 20, transcendentals=3 * total * total // 2
        ),
    )(meta, qkv, grads, tiles)


def by_head(rows):
    return jnp.transpose(rows.reshape(rows.shape[0], -1, HDIM), (1, 0, 2))


def three_parts(x):
    high = lax.reduce_precision(x, 8, 7)
    rest = x - high
    middle = lax.reduce_precision(rest, 8, 7)
    return [high, middle, rest - middle]


def per_device(next_grad, queries, keys, values, outputs, log_sums, part_length):
    devices = lax.axis_size("ctx")
    sections = lax.axis_size("pp")
    ctx = lax.axis_index("ctx")
    tp = lax.axis_index("tp")
    seq, width = queries.shape[1:]
    local_rows = next_grad.shape[1]
    own_cols = lax.dynamic_slice_in_dim(next_grad[0], tp * width, width, 1)
    other_cols = lax.dynamic_slice_in_dim(next_grad[0], (1 - tp) * width, width, 1)
    route = [((p + 1) % sections, p) for p in range(sections)]
    cross = [(2 * a + t, 2 * b + 1 - t) for a, b in route for t in range(2)]
    near = lax.ppermute(own_cols, "pp", route)
    far = lax.ppermute(other_cols, ("pp", "tp"), cross)

    def spread(rows, shared_half):
        heads = by_head(rows)
        shared = heads[devices:]
        if shared_half:
            return heads[:devices], shared.reshape(devices, seq // 2, HDIM)
        return heads[:devices], jnp.repeat(shared, 2, axis=0)

    q_whole, q_shared = spread(queries[0], False)
    k_whole, k_shared = spread(keys[0], True)
    v_whole, v_shared = spread(values[0], True)
    packed = jnp.concatenate([q_whole, k_whole, v_whole, q_shared, k_shared, v_shared], axis=1)
    qkv = lax.all_to_all(packed, "ctx", 0, 0, tiled=True)

    first = jnp.where(tp == 0, near, far)
    second = jnp.where(tp == 0, far, near)
    grad_rows = jnp.concatenate([first, second], axis=0)
    heads = width // HDIM
    deltas = jnp.sum(
        (grad_rows.astype(jnp.float32) * outputs[0].astype(jnp.float32)).reshape(seq, heads, HDIM), axis=2
    )
    g_whole, g_shared = spread(grad_rows, False)

    def stat_rows(x):
        x = jnp.transpose(x)
        both = [x[:devices], jnp.repeat(x[devices:], 2, axis=0)]
        return [jnp.stack(three_parts(y), axis=1) for y in both]

    l_whole, l_shared = stat_rows(log_sums[0] * LOG2E)
    d_whole, d_shared = stat_rows(deltas)
    stats = jnp.concatenate([l_whole, d_whole, l_shared, d_shared], axis=1)
    stats = jnp.pad(stats, ((0, 0), (0, 4), (0, 0))).astype(jnp.bfloat16)
    packed = jnp.concatenate([g_whole, g_shared, stats], axis=1)
    grads = lax.all_to_all(packed, "ctx", 0, 0, tiled=True)
    parts = grads[:, 2 * seq : 2 * seq + 12, :].astype(jnp.float32).reshape(devices, 4, 3, seq)
    stat = jnp.transpose(parts[:, :, 0] + parts[:, :, 1] + parts[:, :, 2], (1, 0, 2)).reshape(4, devices * seq)

    meta = jnp.stack([part_length[0], ctx % 2])
    mixed = attention(meta, qkv, grads, stat)
    back = lax.all_to_all(mixed, "ctx", 0, 0, tiled=True)

    def gather(whole, shared):
        joined = jnp.concatenate([whole, shared], axis=0)
        return jnp.transpose(joined, (1, 0, 2)).reshape(1, seq, width)

    halves = back[:, 3 * seq : 4 * seq].astype(jnp.float32).reshape(devices // 2, 2, seq, HDIM)
    dq_shared = (halves[:, 0] + halves[:, 1]).astype(jnp.bfloat16)
    dk_shared = back[:, 4 * seq : 4 * seq + seq // 2].reshape(devices // 2, seq, HDIM)
    dv_shared = back[:, 4 * seq + seq // 2 :].reshape(devices // 2, seq, HDIM)
    return (
        gather(back[:, :seq], dq_shared),
        gather(back[:, seq : 2 * seq], dk_shared),
        gather(back[:, 2 * seq : 3 * seq], dv_shared),
    )


def solution(mesh):
    rows = P("pp", "ctx", "tp")
    return jax.shard_map(
        per_device,
        mesh=mesh,
        in_specs=(P("pp", ("ctx", "tp"), None), rows, rows, rows, rows, rows, P("pp")),
        out_specs=(rows, rows, rows),
        check_vma=False,
    )
```

time: 491 us -> 164 us (0.33)
  waiting for transfers between devices: 214 us -> 52.2 us
  matrix products: 101 us -> 0 us
  other arithmetic: 40.9 us -> 4.07 us
  blocking collectives: 66.7 us -> 42.2 us
  Pallas kernels: 0 us -> 23.3 us
  local copies, waits for them, and re-layouts: 49 us -> 27.8 us
  between operations: 16.5 us -> 1.68 us
  starting transfers between devices: 0.41 us -> 12.6 us
    all_gather x4 -> x0, waiting for transfers between devices: 204 us -> none  [the longest x1 91.5 us: per_device(): grad_piece = lax.all_gather(grad_rows, 'ctx', axis=0, tiled=True)]
    dot_general x6 -> x0, matrix products: 101 us -> none  [the longest x2 36 us: tile_terms(): jnp.einsum('qhd,khd->hqk', grad_tile, value_tile, preferred_element_type=...]
    all_gather x2 -> x0, blocking collectives: 52.3 us -> none  [the longest x1 26.8 us: per_device(): lax.all_gather(sum_rows, 'ctx', axis=0, tiled=True)]
    all_to_all x0 -> x2, waiting for transfers between devices: none -> 50.5 us  [the longest x1 37.1 us: per_device(): qkv = lax.all_to_all(packed, 'ctx', 0, 0, tiled=True)]
    unnamed x2 -> x0, other arithmetic: 35.8 us -> none
    all_to_all x1, blocking collectives: 14.3 us -> 42.2 us  [per_device(): back = lax.all_to_all(mixed, 'ctx', 0, 0, tiled=True)]
    pallas_call x0 -> x1, Pallas kernels: none -> 23.3 us  [attention(): pl.pallas_call(functools.partial(attention_kernel, blocks=blocks, seq=seq...]
    another operation x3 -> x10, local copies, waits for them, and re-layouts: 16.8 us -> 1.22 us  [the longest x3 1.16 us: by_head(): return jnp.transpose(rows.reshape(rows.shape[0], -1, HDIM), (1, 0, 2))]
  transfers between devices with their start and end apart: 5 -> 4, of which waited for: 4 -> 3; matrix products, arithmetic and copies ran while one was open for 21% -> 9% of each run, Pallas kernels for 0% -> 0%
where the time goes in v1:
time: 164 us
  waiting for transfers between devices  52.2 us (32%)
  blocking collectives  42.2 us (26%)
  local copies, waits for them, and re-layouts  27.8 us (17%)
  Pallas kernels  23.3 us (14%)
  starting transfers between devices  12.6 us (8%)
  other arithmetic  4.07 us (2%)
  between operations  1.68 us (1%)
    all_to_all x1, blocking collectives, per_device(): back = lax.all_to_all(mixed, 'ctx', 0, 0, tiled=True)  42.2 us
    all_to_all x1, waiting for transfers between devices, per_device(): qkv = lax.all_to_all(packed, 'ctx', 0, 0, tiled=True)  37.1 us
    pallas_call x1, Pallas kernels, attention(): pl.pallas_call(functools.partial(attention_kernel, blocks=blocks, seq=seq...  23.3 us
    all_to_all x1, waiting for transfers between devices, per_device(): grads = lax.all_to_all(packed, 'ctx', 0, 0, tiled=True)  13.3 us
    unnamed x29, local copies, waits for them, and re-layouts  12.4 us
    all_to_all x1, starting transfers between devices, per_device(): grads = lax.all_to_all(packed, 'ctx', 0, 0, tiled=True)  7.88 us
    all_to_all x1, starting transfers between devices, per_device(): qkv = lax.all_to_all(packed, 'ctx', 0, 0, tiled=True)  4.46 us
  transfers between devices with their start and end apart: 4, of which 3 were waited for; matrix products, arithmetic and copies ran while one was open for 9% of the time, Pallas kernels for 0%

profile of v1, /device:TPU:24, one launch (start us, length us, event | category | flops | bytes accessed | tf_op | source)
XLA Modules:
  0.0 163.8 jit_solution(18229568460602252684)
XLA Ops:
  0.6 2.1 %dynamic-slice_bitcast_fusion.1 = (bf16[64,3072]{1,0:T(8,128)(2,1)}, bf16[64,3072]{1,0:T(8,128)(2,1)}) fusion(bf16[1,64,6144]{2,1,0:T(8,128)(2,1)} %param.7, s32[]{:T(128)S(6)} %select_n.27, s32[]{:T(128)S(6)} %select_n.28), kind=kLoop, calls=%fused_computation.18 | loop fusion | bytes 1572872 | tf_op jit(solution)/shard_map/dynamic_slice | solution.py:123
  3.0 1.5 copy.117
  4.5 0.4 copy.118
  5.3 0.4 copy.120
  5.7 1.5 copy.121
  7.7 0.8 slice.100
  8.4 0.7 slice.101
  9.2 1.4 copy.144
  10.6 1.7 %collective-permute-done = bf16[64,3072]{1,0:T(8,128)(2,1)} collective-permute-done((bf16[64,3072]{1,0:T(8,128)(2,1)}, bf16[64,3072]{1,0:T(8,128)(2,1)}, u32[]{:S(2)}, u32[]{:S(2)}) %collective-permute-start) | collective-permute-done | bytes 393248 | tf_op jit(solution)/shard_map/ppermute | solution.py:127
  12.4 2.2 %copy.123 = bf16[64,3072]{0,1:T(8,128)(2,1)} copy(bf16[64,3072]{1,0:T(8,128)(2,1)} %collective-permute-done) | data formatting | bytes 786432 | tf_op jit(solution)/shard_map/ppermute | solution.py:127
  14.5 2.2 %copy.124 = bf16[64,3072]{0,1:T(8,128)(2,1)} copy(bf16[64,3072]{1,0:T(8,128)(2,1)} %collective-permute-done.1) | data formatting | bytes 786432 | tf_op jit(solution)/shard_map/ppermute | solution.py:128
  16.7 1.5 broadcast_select_fusion.1
  18.2 0.5 multiply_reduce_fusion
  18.7 0.4 pad_maximum_fusion
  20.0 1.1 fusion.1
  21.2 7.9 %all-to-all-start.1 = ((bf16[16,272,128]{2,1,0:T(8,128)(2,1)}), bf16[16,272,128]{2,1,0:T(8,128)(2,1)S(1)}, u32[]{:S(2)}, u32[]{:S(2)}) async-start(bf16[16,272,128]{2,1,0:T(8,128)(2,1)} %fusion.1), calls=%async_computation.1 | async-start | bytes 2228224 | tf_op jit(solution)/shard_map/all_to_all | solution.py:162
  29.1 0.9 slice_dynamic-update-slice_fusion.2
  29.9 0.9 slice_dynamic-update-slice_fusion.1
  30.8 0.9 slice_dynamic-update-slice_fusion
  31.8 0.9 constant_dynamic-update-slice_fusion.2
  32.7 0.8 constant_dynamic-update-slice_fusion.1
  33.5 0.8 constant_dynamic-update-slice_fusion
  34.3 13.3 %all-to-all-done.1.grads = bf16[16,272,128]{2,1,0:T(8,128)(2,1)S(1)} async-done(((bf16[16,272,128]{2,1,0:T(8,128)(2,1)}), bf16[16,272,128]{2,1,0:T(8,128)(2,1)S(1)}, u32[]{:S(2)}, u32[]{:S(2)}) %all-to-all-start.1) | async-done | bytes 1114144 | tf_op jit(solution)/shard_map/all_to_all | solution.py:162
  47.6 4.5 %all-to-all-start = ((bf16[16,640,128]{2,1,0:T(8,128)(2,1)}), bf16[16,640,128]{2,1,0:T(8,128)(2,1)}, u32[]{:S(2)}, u32[]{:S(2)}) async-start(bf16[16,640,128]{2,1,0:T(8,128)(2,1)} %constant_dynamic-update-slice_fusion), calls=%async_computation | async-start | bytes 5242880 | tf_op jit(solution)/shard_map/all_to_all | solution.py:141
  52.9 37.1 %all-to-all-done.qkv = bf16[16,640,128]{2,1,0:T(8,128)(2,1)} async-done(((bf16[16,640,128]{2,1,0:T(8,128)(2,1)}), bf16[16,640,128]{2,1,0:T(8,128)(2,1)}, u32[]{:S(2)}, u32[]{:S(2)}) %all-to-all-start) | async-done | bytes 2621472 | tf_op jit(solution)/shard_map/all_to_all | solution.py:141
  90.1 23.3 %shard_map.94 = bf16[16,640,128]{2,1,0:T(8,128)(2,1)S(1)} custom-call(s32[2]{0:T(128)S(1)} %pad_add_fusion.meta_ref, bf16[16,640,128]{2,1,0:T(8,128)(2,1)} %all-to-all-done.qkv, bf16[16,272,128]{2,1,0:T(8,128)(2,1)S(1)} %all-to-all-done.1.grads, f32[4,4,512]{2,1,0:T(4,128)S(1)} %reshape_reshape.3.stat), custom_call_target="tpu_custom_call" | custom-call | flops 8053063680 | bytes 8388608 | tf_op jit(solution)/shard_map/pallas_call | solution.py:88
  113.3 42.2 %all_to_all.15 = bf16[16,640,128]{2,1,0:T(8,128)(2,1)S(1)} all-to-all(bf16[16,640,128]{2,1,0:T(8,128)(2,1)S(1)} %shard_map.94), channel_id=1, replica_groups=mesh['ctx'=16,'pp'=4,'tp'=2] {'ctx'}, dimensions={0} | all-to-all | bytes 5242880 | tf_op jit(solution)/shard_map/all_to_all | solution.py:168
  155.5 1.2 fusion.16
  156.9 1.2 copy.138
  158.1 2.3 %copy.141 = bf16[1,128,3072]{2,1,0:T(8,128)(2,1)} copy(bf16[1,128,3072]{1,2,0:T(8,128)(2,1)} %bitcast.84) | data formatting | bytes 1572864
  161.0 1.2 copy.142
  162.6 1.2 copy.143
  (58 shorter events, 3.3 us)
Async XLA Ops:
  0.6 4.3 %copy-start.6 = (bf16[1,128,3072]{2,1,0:T(8,128)(2,1)S(1)}, bf16[1,128,3072]{2,1,0:T(8,128)(2,1)}, u32[]{:S(2)}) copy-start(bf16[1,128,3072]{2,1,0:T(8,128)(2,1)} %param.9) | copy-start | bytes 2359300
  2.8 9.6 %collective-permute-start = (bf16[64,3072]{1,0:T(8,128)(2,1)}, bf16[64,3072]{1,0:T(8,128)(2,1)}, u32[]{:S(2)}, u32[]{:S(2)}) collective-permute-start(bf16[64,3072]{1,0:T(8,128)(2,1)} %get-tuple-element.26), channel_id=1, source_target_pairs={{2,0},{4,2},{6,4},{0,6},{3,1},{5,3},{7,5},{1,7},{10,8},{12,10},{14... | collective-permute-start | bytes 1179656 | tf_op jit(solution)/shard_map/ppermute | solution.py:127
  2.9 11.6 %collective-permute-start.1 = (bf16[64,3072]{1,0:T(8,128)(2,1)}, bf16[64,3072]{1,0:T(8,128)(2,1)}, u32[]{:S(2)}, u32[]{:S(2)}) collective-permute-start(bf16[64,3072]{1,0:T(8,128)(2,1)} %get-tuple-element.27), channel_id=1, source_target_pairs={{2,1},{3,0},{4,3},{5,2},{6,5},{7,4},{0,7},{1,6},{10,9},{11,8},{12,... | collective-permute-start | bytes 1179656 | tf_op jit(solution)/shard_map/ppermute | solution.py:128
  5.7 3.4 %copy-start.8 = (f32[1,128,24]{1,2,0:T(8,128)S(1)}, f32[1,128,24]{1,2,0:T(8,128)}, u32[]{:S(2)}) copy-start(f32[1,128,24]{1,2,0:T(8,128)} %param.12) | copy-start | bytes 36868
  7.6 1.6 copy-start
  9.2 7.5 %copy-start.7 = (f32[24,128]{1,0:T(8,128)}, f32[24,128]{1,0:T(8,128)S(1)}, u32[]{:S(2)}) copy-start(f32[24,128]{1,0:T(8,128)S(1)} %multiply_bitcast_fusion) | copy-start | bytes 36868
  18.7 1.0 slice-start
  21.2 26.5 %all-to-all-start.1 = ((bf16[16,272,128]{2,1,0:T(8,128)(2,1)}), bf16[16,272,128]{2,1,0:T(8,128)(2,1)S(1)}, u32[]{:S(2)}, u32[]{:S(2)}) async-start(bf16[16,272,128]{2,1,0:T(8,128)(2,1)} %fusion.1), calls=%async_computation.1 | async-start | bytes 2228224 | tf_op jit(solution)/shard_map/all_to_all | solution.py:162
  29.0 1.8 %copy-start.1 = (bf16[128,24,128]{2,0,1:T(8,128)(2,1)S(1)}, bf16[128,24,128]{2,0,1:T(8,128)(2,1)}, u32[]{:S(2)}) copy-start(bf16[128,24,128]{2,0,1:T(8,128)(2,1)} %copy-done) | copy-start | bytes 2359300
  29.9 2.8 %copy-start.5 = (bf16[8,128,128]{2,1,0:T(8,128)(2,1)S(1)}, bf16[8,128,128]{2,1,0:T(8,128)(2,1)}, u32[]{:S(2)}) copy-start(bf16[8,128,128]{2,1,0:T(8,128)(2,1)} %slice.100) | copy-start | bytes 786436
  29.9 3.6 %copy-start.4 = (bf16[8,128,128]{2,1,0:T(8,128)(2,1)S(1)}, bf16[8,128,128]{2,1,0:T(8,128)(2,1)}, u32[]{:S(2)}) copy-start(bf16[8,128,128]{2,1,0:T(8,128)(2,1)} %slice.101) | copy-start | bytes 786436
  47.6 42.4 %all-to-all-start = ((bf16[16,640,128]{2,1,0:T(8,128)(2,1)}), bf16[16,640,128]{2,1,0:T(8,128)(2,1)}, u32[]{:S(2)}, u32[]{:S(2)}) async-start(bf16[16,640,128]{2,1,0:T(8,128)(2,1)} %constant_dynamic-update-slice_fusion), calls=%async_computation | async-start | bytes 5242880 | tf_op jit(solution)/shard_map/all_to_all | solution.py:141
  158.1 2.4 %copy-start.3 = (bf16[16,128,128]{2,1,0:T(8,128)(2,1)S(1)}, bf16[16,128,128]{2,1,0:T(8,128)(2,1)}, u32[]{:S(2)}) copy-start(bf16[16,128,128]{2,1,0:T(8,128)(2,1)} %get-tuple-element.19) | copy-start | bytes 1572868
  160.5 1.6 %copy-start.2 = (bf16[16,128,128]{2,1,0:T(8,128)(2,1)S(1)}, bf16[16,128,128]{2,1,0:T(8,128)(2,1)}, u32[]{:S(2)}) copy-start(bf16[16,128,128]{2,1,0:T(8,128)(2,1)} %get-tuple-element.18) | copy-start | bytes 1572868

commit v2 on v1

v2 whole, which is shorter than its diff:
```python
import functools

import jax
import jax.numpy as jnp
from jax import lax
from jax.experimental import pallas as pl
from jax.experimental.pallas import tpu as pltpu
from jax.sharding import PartitionSpec as P

HDIM = 128
LOG2E = 1.4426950408889634
FACTOR = HDIM ** (-0.5)
QTILE = 1024
KTILE = 1024
STAT = 16
VMEM = pl.BlockSpec(memory_space=pltpu.VMEM)
SMEM = pl.BlockSpec(memory_space=pltpu.SMEM)
PARAMS = pltpu.CompilerParams(vmem_limit_bytes=48 << 20)


def dot_nt(a, b):
    return lax.dot_general(a, b, (((1,), (1,)), ((), ())), preferred_element_type=jnp.float32)


def dot_nn(a, b):
    return lax.dot_general(a, b, (((1,), (0,)), ((), ())), preferred_element_type=jnp.float32)


def three_parts(x):
    high = x.astype(jnp.bfloat16).astype(jnp.float32)
    rest = x - high
    middle = rest.astype(jnp.bfloat16).astype(jnp.float32)
    return high, middle, rest - middle


def stat_rows(whole, shared):
    rows = [*whole, *shared, jnp.zeros((STAT - 6, HDIM), jnp.float32)]
    return jnp.concatenate(rows, axis=0).astype(jnp.bfloat16)


def pack_kernel(queries, keys, values, sums, out, *, devices, seq):
    half = seq // 2
    parts = three_parts(sums[...] * LOG2E)
    for d in range(devices):
        whole = slice(d * HDIM, (d + 1) * HDIM)
        head = devices + d // 2
        shared = slice(head * HDIM, (head + 1) * HDIM)
        part = slice((d % 2) * half, (d % 2 + 1) * half)
        out[d, 0:seq, :] = queries[:, whole]
        out[d, seq : 2 * seq, :] = keys[:, whole]
        out[d, 2 * seq : 3 * seq, :] = values[:, whole]
        out[d, 3 * seq : 4 * seq, :] = queries[:, shared]
        out[d, 4 * seq : 4 * seq + half, :] = keys[part, shared]
        out[d, 4 * seq + half : 5 * seq, :] = values[part, shared]
        out[d, 5 * seq : 5 * seq + STAT, :] = stat_rows([x[d : d + 1] for x in parts], [x[head : head + 1] for x in parts])


def pack_grads_kernel(meta, near, far, outputs, out, deltas, *, devices, seq):
    half = seq // 2
    tp = meta[2]
    low = pl.ds(pl.multiple_of(tp * half, half), half)
    high = pl.ds(pl.multiple_of((1 - tp) * half, half), half)
    for d in range(devices):
        head = devices + d // 2
        for at, h in ((0, d), (seq, head)):
            cols = slice(h * HDIM, (h + 1) * HDIM)
            if at == 0 or d % 2 == 0:
                out[d, pl.ds(at + pl.multiple_of(tp * half, half), half), :] = near[:, cols]
                out[d, pl.ds(at + pl.multiple_of((1 - tp) * half, half), half), :] = far[:, cols]
                grad_rows = out[d, at : at + seq, :]
                terms = grad_rows.astype(jnp.float32) * outputs[:, cols].astype(jnp.float32)
                deltas[h : h + 1, :] = jnp.sum(terms.T, axis=0, keepdims=True)
            else:
                out[d, at : at + seq, :] = out[d - 1, at : at + seq, :]
    parts = three_parts(deltas[...])
    for d in range(devices):
        head = devices + d // 2
        out[d, 2 * seq : 2 * seq + STAT, :] = stat_rows([x[d : d + 1] for x in parts], [x[head : head + 1] for x in parts])


def attention_kernel(meta, qkv, grads, stat, out, dq_acc, dk_acc, dv_acc, *, blocks, seq, shared):
    half = seq // 2
    part_len = meta[0]
    which = meta[1]
    span = QTILE // seq
    if shared:
        rows, q_at, k_at, v_at, g_at = half, 3 * seq, 4 * seq, 4 * seq + half, seq
    else:
        rows, q_at, k_at, v_at, g_at = seq, 0, seq, 2 * seq, 0
    dq_at, dk_at, dv_at = 0, seq, seq + rows
    key_span = KTILE // rows
    dq_acc[...] = jnp.zeros_like(dq_acc)

    def key_tile(kt, carry):
        first = kt * key_span
        key_rows = qkv[pl.ds(first, key_span), k_at : k_at + rows, :].reshape(KTILE, HDIM)
        value_rows = qkv[pl.ds(first, key_span), v_at : v_at + rows, :].reshape(KTILE, HDIM)
        key_cols = key_rows.T
        index = lax.broadcasted_iota(jnp.int32, (KTILE, 1), 0)
        if shared:
            key_pos = (first + index // rows) * seq + which * rows + index % rows
        else:
            key_pos = first * seq + index
        key_pos = jnp.where(key_pos < part_len, -1, key_pos)
        dk_acc[...] = jnp.zeros_like(dk_acc)
        dv_acc[...] = jnp.zeros_like(dv_acc)

        def query_tile(qt, carry):
            at = qt * span
            query_rows = qkv[pl.ds(at, span), q_at : q_at + seq, :].reshape(QTILE, HDIM)
            grad_rows = grads[pl.ds(at, span), g_at : g_at + seq, :].reshape(QTILE, HDIM)
            log_sum = stat[0, pl.ds(qt, 1), :]
            delta = stat[1, pl.ds(qt, 1), :]
            scores = dot_nt(key_rows, query_rows) * (FACTOR * LOG2E) - log_sum
            query_pos = at * seq + lax.broadcasted_iota(jnp.int32, (1, QTILE), 1)
            weights = jnp.where(key_pos <= query_pos, jnp.exp2(scores), 0.0)
            weight_grads = dot_nt(value_rows, grad_rows)
            score_grads = (weights * (weight_grads - delta) * FACTOR).astype(jnp.bfloat16)
            dv_acc[...] += dot_nn(weights.astype(jnp.bfloat16), grad_rows)
            dk_acc[...] += dot_nn(score_grads, query_rows)
            where = pl.ds(pl.multiple_of(at * seq, QTILE), QTILE)
            dq_acc[:, where] += dot_nn(key_cols, score_grads)
            return carry

        lax.fori_loop(0, blocks // span, query_tile, 0)
        shape = (key_span, rows, HDIM)
        out[pl.ds(first, key_span), dk_at : dk_at + rows, :] = dk_acc[...].astype(jnp.bfloat16).reshape(shape)
        out[pl.ds(first, key_span), dv_at : dv_at + rows, :] = dv_acc[...].astype(jnp.bfloat16).reshape(shape)
        return carry

    lax.fori_loop(0, blocks // key_span, key_tile, 0)
    for b in range(blocks):
        out[b, dq_at : dq_at + seq, :] = dq_acc[:, b * seq : (b + 1) * seq].T.astype(jnp.bfloat16)


def attention(meta, qkv, grads, stat, seq, shared):
    blocks = qkv.shape[0]
    total = blocks * seq
    keys = total // 2 if shared else total
    out_rows = 2 * seq if shared else 3 * seq
    return pl.pallas_call(
        functools.partial(attention_kernel, blocks=blocks, seq=seq, shared=shared),
        out_shape=jax.ShapeDtypeStruct((blocks, out_rows, HDIM), jnp.bfloat16),
        in_specs=[SMEM, VMEM, VMEM, VMEM],
        out_specs=VMEM,
        scratch_shapes=[
            pltpu.VMEM((HDIM, total), jnp.float32),
            pltpu.VMEM((KTILE, HDIM), jnp.float32),
            pltpu.VMEM((KTILE, HDIM), jnp.float32),
        ],
        compiler_params=PARAMS,
        cost_estimate=pl.CostEstimate(
            flops=10 * total * keys * HDIM, bytes_accessed=4 << 20, transcendentals=total * keys
        ),
        name="shared_head" if shared else "whole_head",
    )(meta, qkv, grads, stat.reshape(2, total // QTILE, QTILE))


def unpack_kernel(whole, shared, dq, dk, dv, *, devices, seq):
    half = seq // 2
    for d in range(devices):
        cols = slice(d * HDIM, (d + 1) * HDIM)
        dq[:, cols] = whole[d, 0:seq, :]
        dk[:, cols] = whole[d, seq : 2 * seq, :]
        dv[:, cols] = whole[d, 2 * seq : 3 * seq, :]
        head = devices + d // 2
        cols = slice(head * HDIM, (head + 1) * HDIM)
        if d % 2 == 0:
            both = shared[d, 0:seq, :].astype(jnp.float32) + shared[d + 1, 0:seq, :].astype(jnp.float32)
            dq[:, cols] = both.astype(jnp.bfloat16)
        part = slice((d % 2) * half, (d % 2 + 1) * half)
        dk[part, cols] = shared[d, seq : seq + half, :]
        dv[part, cols] = shared[d, seq + half : 2 * seq, :]


def joined_stat(rows):
    devices, _, seq = rows.shape
    x = rows[:, :6].astype(jnp.float32).reshape(devices, 2, 3, seq)
    x = x[:, :, 0] + x[:, :, 1] + x[:, :, 2]
    return jnp.transpose(x, (1, 0, 2)).reshape(2, devices * seq)


def per_device(next_grad, queries, keys, values, outputs, log_sums, part_length):
    devices = lax.axis_size("ctx")
    sections = lax.axis_size("pp")
    ctx = lax.axis_index("ctx")
    tp = lax.axis_index("tp")
    seq, width = queries.shape[1:]
    meta = jnp.stack([part_length[0], ctx % 2, tp])
    sizes = dict(devices=devices, seq=seq)

    packed = pl.pallas_call(
        functools.partial(pack_kernel, **sizes),
        out_shape=jax.ShapeDtypeStruct((devices, 5 * seq + STAT, HDIM), jnp.bfloat16),
        in_specs=[VMEM] * 4,
        out_specs=VMEM,
        compiler_params=PARAMS,
        name="pack",
    )(queries[0], keys[0], values[0], jnp.transpose(log_sums[0]))
    qkv = lax.all_to_all(packed, "ctx", 0, 0, tiled=True)

    own_cols = lax.dynamic_slice_in_dim(next_grad[0], tp * width, width, 1)
    other_cols = lax.dynamic_slice_in_dim(next_grad[0], (1 - tp) * width, width, 1)
    route = [((p + 1) % sections, p) for p in range(sections)]
    cross = [(2 * a + t, 2 * b + 1 - t) for a, b in route for t in range(2)]
    near = lax.ppermute(own_cols, "pp", route)
    far = lax.ppermute(other_cols, ("pp", "tp"), cross)
    packed_grads = pl.pallas_call(
        functools.partial(pack_grads_kernel, **sizes),
        out_shape=jax.ShapeDtypeStruct((devices, 2 * seq + STAT, HDIM), jnp.bfloat16),
        in_specs=[SMEM] + [VMEM] * 3,
        out_specs=VMEM,
        scratch_shapes=[pltpu.VMEM((width // HDIM, seq), jnp.float32)],
        compiler_params=PARAMS,
        name="pack_grads",
    )(meta, near, far, outputs[0])
    packed_grads, qkv = lax.optimization_barrier((packed_grads, qkv))
    grads = lax.all_to_all(packed_grads, "ctx", 0, 0, tiled=True)

    sums = joined_stat(qkv[:, 5 * seq :])
    deltas = joined_stat(grads[:, 2 * seq :])
    stat = jnp.stack([sums, deltas], axis=1)
    mixed = attention(meta, qkv, grads, stat[1], seq, True)
    back_shared = lax.all_to_all(mixed, "ctx", 0, 0, tiled=True)
    mixed = attention(meta, qkv, grads, stat[0], seq, False)
    back_whole = lax.all_to_all(mixed, "ctx", 0, 0, tiled=True)

    result = jax.ShapeDtypeStruct((seq, width), jnp.bfloat16)
    dq, dk, dv = pl.pallas_call(
        functools.partial(unpack_kernel, **sizes),
        out_shape=(result, result, result),
        in_specs=[VMEM] * 2,
        out_specs=(VMEM,) * 3,
        compiler_params=PARAMS,
        name="unpack",
    )(back_whole, back_shared)
    return dq[None], dk[None], dv[None]


def solution(mesh):
    rows = P("pp", "ctx", "tp")
    return jax.shard_map(
        per_device,
        mesh=mesh,
        in_specs=(P("pp", ("ctx", "tp"), None), rows, rows, rows, rows, rows, P("pp")),
        out_specs=(rows, rows, rows),
        check_vma=False,
    )
```

time: 164 us -> 133 us (0.81)
  local copies, waits for them, and re-layouts: 27.8 us -> 9.01 us
  blocking collectives: 42.2 us -> 27.4 us
  Pallas kernels: 23.3 us -> 27.8 us
  starting transfers between devices: 12.6 us -> 17 us
  waiting for transfers between devices: 52.2 us -> 48.3 us
  other arithmetic: 4.07 us -> 0.9 us
    all_to_all x1, waiting for transfers between devices: 37.1 us -> 21.4 us  [per_device(): qkv = lax.all_to_all(packed, 'ctx', 0, 0, tiled=True)]
    all_to_all x1, blocking collectives: 42.2 us -> 27.4 us  [per_device(): back_whole = lax.all_to_all(mixed, 'ctx', 0, 0, tiled=True)]
    ppermute x1, waiting for transfers between devices: 0.01 us -> 10.1 us  [per_device(): far = lax.ppermute(other_cols, ('pp', 'tp'), cross)]
    pallas_call x0 -> x3, Pallas kernels: none -> 6.67 us  [the longest x1 2.7 us: per_device(): pl.pallas_call(functools.partial(pack_grads_kernel, **sizes), out_shape=j...]
    unnamed x29 -> x16, local copies, waits for them, and re-layouts: 12.4 us -> 6.81 us
    ppermute x2 -> x0, local copies, waits for them, and re-layouts: 4.3 us -> none  [the longest x1 2.15 us: per_device(): far = lax.ppermute(other_cols, ('pp', 'tp'), cross)]
    all_to_all x1 -> x2, waiting for transfers between devices: 13.3 us -> 16.9 us  [the longest x1 16.4 us: per_device(): grads = lax.all_to_all(packed_grads, 'ctx', 0, 0, tiled=True)]
    all_to_all x1, starting transfers between devices: 4.46 us -> 7.88 us  [per_device(): qkv = lax.all_to_all(packed, 'ctx', 0, 0, tiled=True)]
  transfers between devices with their start and end apart: 4 -> 5, of which waited for: 3 -> 4; matrix products, arithmetic and copies ran while one was open for 9% -> 2% of each run, Pallas kernels for 0% -> 12%
where the time goes in v2:
time: 133 us; the launch traced here: 132 us
  waiting for transfers between devices  48.3 us (36%)
  Pallas kernels  27.8 us (21%)
  blocking collectives  27.4 us (21%)
  starting transfers between devices  17 us (13%)
  local copies, waits for them, and re-layouts  9.01 us (7%)
  between operations  1.43 us (1%)
    all_to_all x1, blocking collectives, per_device(): back_whole = lax.all_to_all(mixed, 'ctx', 0, 0, tiled=True)  27.4 us
    all_to_all x1, waiting for transfers between devices, per_device(): qkv = lax.all_to_all(packed, 'ctx', 0, 0, tiled=True)  21.4 us
    pallas_call x2, Pallas kernels, attention(): pl.pallas_call(functools.partial(attention_kernel, blocks=blocks, seq=seq...  21.1 us
    all_to_all x1, waiting for transfers between devices, per_device(): grads = lax.all_to_all(packed_grads, 'ctx', 0, 0, tiled=True)  16.4 us
    ppermute x1, waiting for transfers between devices, per_device(): far = lax.ppermute(other_cols, ('pp', 'tp'), cross)  10.1 us
    all_to_all x1, starting transfers between devices, per_device(): qkv = lax.all_to_all(packed, 'ctx', 0, 0, tiled=True)  7.88 us
    unnamed x16, local copies, waits for them, and re-layouts  6.81 us
    all_to_all x1, starting transfers between devices, per_device(): grads = lax.all_to_all(packed_grads, 'ctx', 0, 0, tiled=True)  4.62 us
  transfers between devices with their start and end apart: 5, of which 4 were waited for; matrix products, arithmetic and copies ran while one was open for 2% of the time, Pallas kernels for 12%

profile of v2, /device:TPU:24, one launch (start us, length us, event | category | flops | bytes accessed | tf_op | source)
XLA Modules:
  0.0 131.8 jit_solution(2640773619358484099)
XLA Ops:
  0.6 0.0 copy-start.4
  0.6 1.1 copy-done.4
  1.8 0.0 copy-start.5
  1.8 1.1 copy-done.5
  2.9 1.1 copy-done.6
  4.0 0.7 copy-done.7
  4.7 2.0 %pack.1 = bf16[16,656,128]{2,1,0:T(8,128)(2,1)} custom-call(bf16[128,3072]{1,0:T(8,128)(2,1)S(1)} %bitcast.29, bf16[128,3072]{1,0:T(8,128)(2,1)S(1)} %bitcast.30, bf16[128,3072]{1,0:T(8,128)(2,1)S(1)} %bitcast.31, f32[24,128]{1,0:T(8,128)S(1)} %bitcast.32), custom_call_target="tpu_custom_call" | custom-call | tf_op jit(solution)/shard_map/pack/pallas_call | solution.py:192
  6.7 7.9 %all-to-all-start = ((bf16[16,656,128]{2,1,0:T(8,128)(2,1)}), bf16[16,656,128]{2,1,0:T(8,128)(2,1)S(1)}, u32[]{:S(2)}, u32[]{:S(2)}) async-start(bf16[16,656,128]{2,1,0:T(8,128)(2,1)} %pack.1), calls=%async_computation | async-start | bytes 5373952 | tf_op jit(solution)/shard_map/all_to_all | solution.py:200
  14.6 0.0 copy-start.3
  14.6 2.1 %dynamic-slice_bitcast_fusion = (bf16[64,3072]{1,0:T(8,128)(2,1)}, bf16[64,3072]{1,0:T(8,128)(2,1)}) fusion(bf16[1,64,6144]{2,1,0:T(8,128)(2,1)} %param.7, s32[]{:T(128)S(6)} %select_n.15, s32[]{:T(128)S(6)} %select_n.14), kind=kLoop, calls=%fused_computation | loop fusion | bytes 1572872 | tf_op jit(solution)/shard_map/dynamic_slice | solution.py:203
  16.7 0.0 collective-permute-start.1
  16.7 0.8 collective-permute-start
  18.2 0.1 pad_add_fusion.meta
  18.3 10.1 %collective-permute-done.1.far = bf16[64,3072]{1,0:T(8,128)(2,1)} collective-permute-done((bf16[64,3072]{1,0:T(8,128)(2,1)}, bf16[64,3072]{1,0:T(8,128)(2,1)}, u32[]{:S(2)}, u32[]{:S(2)}) %collective-permute-start.1) | collective-permute-done | bytes 393248 | tf_op jit(solution)/shard_map/ppermute | solution.py:207
  28.4 0.0 collective-permute-done.near
  28.4 0.0 copy-done.3
  28.4 2.7 %pack_grads.1 = bf16[16,272,128]{2,1,0:T(8,128)(2,1)} custom-call(s32[3]{0:T(128)S(1)} %pad_add_fusion.meta, bf16[64,3072]{1,0:T(8,128)(2,1)} %collective-permute-done.near, bf16[64,3072]{1,0:T(8,128)(2,1)} %collective-permute-done.1.far, bf16[128,3072]{1,0:T(8,128)(2,1)S(1)} %bitcast.28), custom_call_target="tpu_custom_call" | custom-call | tf_op jit(solution)/shard_map/pack_grads/pallas_call | solution.py:208
  31.1 21.4 %all-to-all-done.qkv = bf16[16,656,128]{2,1,0:T(8,128)(2,1)S(1)} async-done(((bf16[16,656,128]{2,1,0:T(8,128)(2,1)}), bf16[16,656,128]{2,1,0:T(8,128)(2,1)S(1)}, u32[]{:S(2)}, u32[]{:S(2)}) %all-to-all-start) | async-done | bytes 2687008 | tf_op jit(solution)/shard_map/all_to_all | solution.py:200
  52.5 4.6 %all-to-all-start.1 = ((bf16[16,272,128]{2,1,0:T(8,128)(2,1)}), bf16[16,272,128]{2,1,0:T(8,128)(2,1)}, u32[]{:S(2)}, u32[]{:S(2)}) async-start(bf16[16,272,128]{2,1,0:T(8,128)(2,1)} %pack_grads.1), calls=%async_computation.1 | async-start | bytes 2228224 | tf_op jit(solution)/shard_map/all_to_all | solution.py:218
  57.1 16.4 %all-to-all-done.1.grads = bf16[16,272,128]{2,1,0:T(8,128)(2,1)} async-done(((bf16[16,272,128]{2,1,0:T(8,128)(2,1)}), bf16[16,272,128]{2,1,0:T(8,128)(2,1)}, u32[]{:S(2)}, u32[]{:S(2)}) %all-to-all-start.1) | async-done | bytes 1114144 | tf_op jit(solution)/shard_map/all_to_all | solution.py:218
  73.5 0.8 slice_convert_fusion
  74.4 7.6 %shared_head.1 = bf16[16,256,128]{2,1,0:T(8,128)(2,1)S(1)} custom-call(s32[3]{0:T(128)S(1)} %pad_add_fusion.meta, bf16[16,656,128]{2,1,0:T(8,128)(2,1)S(1)} %all-to-all-done.qkv, bf16[16,272,128]{2,1,0:T(8,128)(2,1)} %all-to-all-done.1.grads, f32[2,2,1024]{2,1,0:T(2,128)S(1)} %reshape_squeeze.7.stat), custom_call_target="tpu_custom_call" | custom-call | flops 2684354560 | bytes 4194304 | tf_op jit(solution)/shard_map/shared_head/pallas_call | solution.py:141
  82.0 0.0 copy-done
  82.0 0.0 copy-start.2
  82.0 1.0 copy-done.2
  83.0 3.7 %all-to-all-start.3 = ((bf16[16,256,128]{2,1,0:T(8,128)(2,1)}), bf16[16,256,128]{2,1,0:T(8,128)(2,1)S(1)}, u32[]{:S(2)}, u32[]{:S(2)}) async-start(bf16[16,256,128]{2,1,0:T(8,128)(2,1)} %copy-done.2), calls=%async_computation.3 | async-start | bytes 2097152 | tf_op jit(solution)/shard_map/all_to_all | solution.py:224
  86.7 0.0 copy-start.1
  86.7 1.7 %copy-done.1 = bf16[16,656,128]{2,1,0:T(8,128)(2,1)S(1)} copy-done((bf16[16,656,128]{2,1,0:T(8,128)(2,1)S(1)}, bf16[16,656,128]{2,1,0:T(8,128)(2,1)}, u32[]{:S(2)}) %copy-start.1) | copy-done | bytes 2687000
  88.4 13.5 %whole_head.1 = bf16[16,384,128]{2,1,0:T(8,128)(2,1)S(1)} custom-call(s32[3]{0:T(128)S(1)} %pad_add_fusion.meta, bf16[16,656,128]{2,1,0:T(8,128)(2,1)S(1)} %copy-done.1, bf16[16,272,128]{2,1,0:T(8,128)(2,1)} %all-to-all-done.1.grads, f32[2,2,1024]{2,1,0:T(2,128)S(1)} %reshape_squeeze.6.stat), custom_call_target="tpu_custom_call" | custom-call | flops 5368709120 | bytes 4194304 | tf_op jit(solution)/shard_map/whole_head/pallas_call | solution.py:141
  101.9 0.5 all-to-all-done.3.shared
  102.4 27.4 %all_to_all.20.whole = bf16[16,384,128]{2,1,0:T(8,128)(2,1)S(1)} all-to-all(bf16[16,384,128]{2,1,0:T(8,128)(2,1)S(1)} %whole_head.1), channel_id=1, replica_groups=mesh['ctx'=16,'pp'=4,'tp'=2] {'ctx'}, dimensions={0} | all-to-all | bytes 3145728 | tf_op jit(solution)/shard_map/all_to_all | solution.py:226
  129.8 2.0 %unpack.1 = (bf16[128,3072]{1,0:T(8,128)(2,1)}, bf16[128,3072]{1,0:T(8,128)(2,1)}, bf16[128,3072]{1,0:T(8,128)(2,1)}) custom-call(bf16[16,384,128]{2,1,0:T(8,128)(2,1)S(1)} %all_to_all.20.whole, bf16[16,256,128]{2,1,0:T(8,128)(2,1)S(1)} %all-to-all-done.3.shared), custom_call_target="tpu_custom_call" | custom-call | tf_op jit(solution)/shard_map/unpack/pallas_call | solution.py:229
  (11 shorter events, 0.1 us)
Async XLA Ops:
  0.6 1.1 copy-start.4
  1.8 1.1 copy-start.5
  2.9 1.1 copy-start.6
  4.0 0.7 copy-start.7
  6.7 45.7 %all-to-all-start = ((bf16[16,656,128]{2,1,0:T(8,128)(2,1)}), bf16[16,656,128]{2,1,0:T(8,128)(2,1)S(1)}, u32[]{:S(2)}, u32[]{:S(2)}) async-start(bf16[16,656,128]{2,1,0:T(8,128)(2,1)} %pack.1), calls=%async_computation | async-start | bytes 5373952 | tf_op jit(solution)/shard_map/all_to_all | solution.py:200
  14.6 13.8 %copy-start.3 = (bf16[1,128,3072]{2,1,0:T(8,128)(2,1)S(1)}, bf16[1,128,3072]{2,1,0:T(8,128)(2,1)}, u32[]{:S(2)}) copy-start(bf16[1,128,3072]{2,1,0:T(8,128)(2,1)} %param.11) | copy-start | bytes 2359300
  16.7 11.6 %collective-permute-start.1 = (bf16[64,3072]{1,0:T(8,128)(2,1)}, bf16[64,3072]{1,0:T(8,128)(2,1)}, u32[]{:S(2)}, u32[]{:S(2)}) collective-permute-start(bf16[64,3072]{1,0:T(8,128)(2,1)} %get-tuple-element.13), channel_id=1, source_target_pairs={{2,1},{3,0},{4,3},{5,2},{6,5},{7,4},{0,7},{1,6},{10,9},{11,8},{12,... | collective-permute-start | bytes 1179656 | tf_op jit(solution)/shard_map/ppermute | solution.py:207
  16.7 11.6 %collective-permute-start = (bf16[64,3072]{1,0:T(8,128)(2,1)}, bf16[64,3072]{1,0:T(8,128)(2,1)}, u32[]{:S(2)}, u32[]{:S(2)}) collective-permute-start(bf16[64,3072]{1,0:T(8,128)(2,1)} %get-tuple-element.14), channel_id=1, source_target_pairs={{2,0},{4,2},{6,4},{0,6},{3,1},{5,3},{7,5},{1,7},{10,8},{12,10},{14... | collective-permute-start | bytes 1179656 | tf_op jit(solution)/shard_map/ppermute | solution.py:206
  52.5 29.5 %copy-start = (bf16[16,656,128]{2,1,0:T(8,128)(2,1)}, bf16[16,656,128]{2,1,0:T(8,128)(2,1)S(1)}, u32[]{:S(2)}) copy-start(bf16[16,656,128]{2,1,0:T(8,128)(2,1)S(1)} %all-to-all-done.qkv) | copy-start | bytes 8060932
  52.5 21.1 %all-to-all-start.1 = ((bf16[16,272,128]{2,1,0:T(8,128)(2,1)}), bf16[16,272,128]{2,1,0:T(8,128)(2,1)}, u32[]{:S(2)}, u32[]{:S(2)}) async-start(bf16[16,272,128]{2,1,0:T(8,128)(2,1)} %pack_grads.1), calls=%async_computation.1 | async-start | bytes 2228224 | tf_op jit(solution)/shard_map/all_to_all | solution.py:218
  82.0 1.0 copy-start.2
  83.0 19.4 %all-to-all-start.3 = ((bf16[16,256,128]{2,1,0:T(8,128)(2,1)}), bf16[16,256,128]{2,1,0:T(8,128)(2,1)S(1)}, u32[]{:S(2)}, u32[]{:S(2)}) async-start(bf16[16,256,128]{2,1,0:T(8,128)(2,1)} %copy-done.2), calls=%async_computation.3 | async-start | bytes 2097152 | tf_op jit(solution)/shard_map/all_to_all | solution.py:224
  86.7 1.8 %copy-start.1 = (bf16[16,656,128]{2,1,0:T(8,128)(2,1)S(1)}, bf16[16,656,128]{2,1,0:T(8,128)(2,1)}, u32[]{:S(2)}) copy-start(bf16[16,656,128]{2,1,0:T(8,128)(2,1)} %copy-done) | copy-start | bytes 8060932
